TPU v7x, 256 devices: a whole 4x4x8 slice. The times are simulated.
256 devices in a mesh: clip: 16 (over z, x_hi), tm: 16 (over x_lo, y, core).
Axes of the slice: x: 4 (x_hi: 2, x_lo: 2; x = x_hi * 2 + x_lo), y: 4, z: 8, core: 2. Of those that a mesh axis runs over, the one named last changes fastest.
Arguments:
- queries: bfloat16 [16, 4096, 1536], P('clip', 'tm'), may hold values from -8 to 8
- key_rows: bfloat16 [16, 4096, 1536], P('clip', 'tm'), may hold values from -8 to 8
- value_rows: bfloat16 [16, 4096, 1536], P('clip', 'tm'), may hold values from -6 to 6
- grad_out: bfloat16 [16, 4096, 1536], P('clip', 'tm'), may hold values from -16 to 16
- query_gain: float32 [128], replicated, may hold values from 0.5 to 5
- key_gain: float32 [128], replicated, may hold values from 0.5 to 5
- valid_frames: int32 [16, 16], P('clip'), may hold values from 1 to 4
- window_start: int32 [16, 64], P('clip'), may hold values from 0 to 2
Outputs:
- attended: bfloat16 [16, 4096, 1536], P('clip', 'tm')
- query_grad: bfloat16 [16, 4096, 1536], P('clip', 'tm')
- key_grad: bfloat16 [16, 4096, 1536], P('clip', 'tm')
- value_grad: bfloat16 [16, 4096, 1536], P('clip', 'tm')
- query_gain_grad: float32 [128], replicated
- key_gain_grad: float32 [128], replicated
All inputs are finite; a program needn't handle non-finite values.
Results may differ from a plain program's by a relative error of at most 0.0045.
The roundings to bfloat16 on the way count: a program that leaves them out, or rounds other values in their place, can miss the bound.
Values may be sent and summed in bfloat16 or wider, within the bound.
A program may use at most 128 MiB of HBM per device.

v0:
```python
import functools
import math

import jax
import jax.numpy as jnp
from jax import lax
from jax.experimental import pallas as pl
from jax.experimental.pallas import tpu as pltpu
from jax.sharding import PartitionSpec as P

MESH = pl.DeviceIdType.MESH
H = 12
HD = 128
GW = 4
WW = 2
TILE = 64
FRAME = 16
TOK = 256
HH = 1536
N_TM = 16
N_CLIP = 16
EPSILON = 1e-06
ROOT = 1.0 / math.sqrt(HD)
SCALE = ROOT * math.log2(math.e)
DEAD = -1e30
GROUPS = 3
PER = H // GROUPS
GCOLS = PER * HD

NT = (((1,), (1,)), ((), ()))
TN = (((0,), (0,)), ((), ()))


def dot(a, b, dims=(((1,), (0,)), ((), ()))):
    return lax.dot_general(a, b, dims, preferred_element_type=jnp.float32)


def cols(h):
    return pl.ds(pl.multiple_of(h * HD, HD), HD)


def group_cols(g):
    return pl.ds(pl.multiple_of(g * GCOLS, GCOLS), GCOLS)


def inv_rms(values):
    return lax.rsqrt(jnp.mean(values * values, axis=-1, keepdims=True) + EPSILON)


def norm_back(values, scale, gain, upstream):
    weighted = gain * upstream
    inner = jnp.mean(values * weighted, axis=-1, keepdims=True)
    return scale * weighted - values * (scale * scale * scale * inner)


def fold(rows):
    return jnp.sum(rows.reshape(TOK // 8, 8, HD), axis=0)


def main_kernel(
    q_hbm, k_hbm, v_hbm, g_hbm, q_gain, k_gain, frames, starts,
    att_out, dq_out, dk_out, dv_out, gains_out,
    raw, halo, qn_own, kn_own, acc, stage, bias_f, bias_b,
    stat_cols, stat_mine, stat_halo, gain_acc, part, ring_in, clip_in, total,
    load_sem, out_sem, send_sem, recv_sem, stat_send, stat_recv,
    ready, ring_send, ring_recv, clip_send, clip_recv, total_send, total_recv,
):
    me = lax.axis_index("tm")
    clip = lax.axis_index("clip")
    has_left = me > 0
    has_right = me < N_TM - 1
    loads = []
    for i, ref in enumerate((q_hbm, k_hbm, v_hbm, g_hbm)):
        load = pltpu.make_async_copy(ref.at[0], raw.at[i], load_sem.at[i])
        load.start()
        loads.append(load)

    barrier = pltpu.get_barrier_semaphore()

    @pl.when(has_left)
    def _():
        pl.semaphore_signal(barrier, inc=1, device_id={"tm": me - 1}, device_id_type=MESH)

    @pl.when(has_right)
    def _():
        pl.semaphore_signal(barrier, inc=1, device_id={"tm": me + 1}, device_id_type=MESH)

    @pl.when(me > 1)
    def _():
        pl.semaphore_signal(barrier, inc=1, device_id={"tm": 0}, device_id_type=MESH)

    @pl.when(me == 0)
    def _():
        for j in range(1, N_CLIP):
            pl.semaphore_signal(
                barrier, inc=1, device_id={"clip": lax.rem(clip + j, N_CLIP)}, device_id_type=MESH
            )
        pl.semaphore_wait(barrier, N_TM - 1 + N_CLIP - 1)
        for i in range(1, N_TM):
            pl.semaphore_signal(ready, inc=1, device_id={"tm": i}, device_id_type=MESH)

    @pl.when(jnp.logical_and(has_left, has_right))
    def _():
        pl.semaphore_wait(barrier, 2)

    @pl.when(me == N_TM - 1)
    def _():
        pl.semaphore_wait(barrier, 1)

    def transfer(side, a, g):
        source = qn_own if a == 3 else (k_hbm, v_hbm, g_hbm)[a].at[0]
        return pltpu.make_async_remote_copy(
            src_ref=source.at[:, group_cols(g)],
            dst_ref=halo.at[1 - side, a, :, group_cols(g)],
            send_sem=send_sem.at[side, a, g],
            recv_sem=recv_sem.at[1 - side, a, g],
            device_id={"tm": me + (1 if side else -1)},
            device_id_type=MESH,
        )

    def stat_transfer(side, g):
        return pltpu.make_async_remote_copy(
            src_ref=stat_mine.at[g],
            dst_ref=stat_halo.at[1 - side, g],
            send_sem=stat_send.at[side, g],
            recv_sem=stat_recv.at[1 - side, g],
            device_id={"tm": me + (1 if side else -1)},
            device_id_type=MESH,
        )

    def send(arrays, g):
        for side, present in ((0, has_left), (1, has_right)):

            @pl.when(present)
            def _():
                for a in arrays:
                    transfer(side, a, g).start()

    def receive(arrays, g):
        for side, present in ((0, has_left), (1, has_right)):

            @pl.when(present)
            def _():
                for a in arrays:
                    transfer(1 - side, a, g).wait_recv()

    for g in range(GROUPS):
        send((0, 1), g)

    for side, present in ((0, has_left), (1, has_right)):

        @pl.when(jnp.logical_not(present))
        def _():
            halo[side] = jnp.zeros((4, TOK, HH), jnp.bfloat16)
            stat_halo[side] = jnp.zeros((GROUPS, 8, TOK), jnp.float32)

    rows = lax.broadcasted_iota(jnp.int32, (TOK, TOK), 0)
    lanes = lax.broadcasted_iota(jnp.int32, (TOK, TOK), 1)

    def window_of(where, position, present):
        chosen = jnp.zeros((TOK, TOK), jnp.int32)
        for t in range(GW):
            start = starts[0, position * GW + t]
            chosen = jnp.where(where // TILE == t, jnp.where(present, start, -100), chosen)
        return chosen

    def bias_of(window, keys, count):
        column = keys // TILE
        frame = (keys % TILE) // FRAME
        live = (column >= window) & (column < window + WW) & (frame < count)
        return jnp.where(live, 0.0, DEAD).astype(jnp.float32)

    before = jnp.maximum(me - 1, 0)
    after = jnp.minimum(me + 1, N_TM - 1)
    mine = window_of(rows, me, me >= 0)
    count_own = frames[0, me]
    bias_f[0] = bias_of(mine, lanes, jnp.where(has_left, frames[0, before], 0))
    bias_f[1] = bias_of(mine, lanes, count_own)
    bias_f[2] = bias_of(mine, lanes, jnp.where(has_right, frames[0, after], 0))
    bias_b[0] = bias_of(window_of(lanes, before, has_left), rows, count_own)
    bias_b[1] = bias_of(window_of(lanes, after, has_right), rows, count_own)

    gain_acc[...] = jnp.zeros_like(gain_acc)
    stat_cols[...] = jnp.zeros_like(stat_cols)
    gain_q = q_gain[...]
    gain_k = k_gain[...]
    ungain_k = 1.0 / gain_k
    for load in loads:
        load.wait()

    def normal_queries(h, carry):
        values = raw[0, :, cols(h)].astype(jnp.float32)
        qn_own[:, cols(h)] = (values * inv_rms(values) * gain_q).astype(jnp.bfloat16)
        return carry

    lax.fori_loop(0, H, normal_queries, 0)

    stat_lane = lax.broadcasted_iota(jnp.int32, (TOK, HD), 1)

    def forward_head(local, g):
        h = g * PER + local
        at = cols(h)
        qn = qn_own[:, at]
        grads = raw[3, :, at]
        keys, extras, values = [], [], []
        for p in range(3):
            rough = (halo[0, 0, :, at], raw[1, :, at], halo[1, 0, :, at])[p].astype(jnp.float32)
            hat = rough * inv_rms(rough)
            kn = (hat * gain_k).astype(jnp.bfloat16)
            keys.append(kn)
            extras.append((hat - kn.astype(jnp.float32) * ungain_k).astype(jnp.bfloat16))
            values.append((halo[0, 1, :, at], raw[2, :, at], halo[1, 1, :, at])[p])
        kn_own[:, at] = keys[1]
        scores = [dot(qn, keys[p], NT) * SCALE + bias_f[p] for p in range(3)]
        peak = jnp.max(jnp.maximum(jnp.maximum(scores[0], scores[1]), scores[2]), axis=-1, keepdims=True)
        weights = [jnp.exp2(s - peak) for s in scores]
        mass = jnp.sum(weights[0] + weights[1] + weights[2], axis=-1, keepdims=True)
        inverse = 1.0 / mass
        probs = [w * inverse for w in weights]
        slopes = [dot(grads, values[p], NT) for p in range(3)]
        delta = jnp.sum(
            probs[0] * slopes[0] + probs[1] * slopes[1] + probs[2] * slopes[2], axis=-1, keepdims=True
        )
        low = [x.astype(jnp.bfloat16) for x in probs]
        change = [(probs[p] * (slopes[p] - delta)).astype(jnp.bfloat16) for p in range(3)]
        stage[0, :, at] = sum(dot(low[p], values[p]) for p in range(3)).astype(jnp.bfloat16)
        wide = sum(
            dot(change[p], jnp.concatenate([keys[p], extras[p]], axis=1)) for p in range(3)
        )
        dqn = wide[:, :HD] * ROOT
        by_hat = dqn * ungain_k + wide[:, HD:] * ROOT
        query = raw[0, :, at].astype(jnp.float32)
        scale = inv_rms(query)
        gain_acc[0] += fold(dqn * query * scale)
        gain_acc[1] += fold(qn.astype(jnp.float32) * by_hat)
        stage[1, :, at] = norm_back(query, scale, gain_q, dqn).astype(jnp.bfloat16)
        acc[0, :, at] = dot(change[1], qn, TN)
        acc[1, :, at] = dot(low[1], grads, TN)
        logs = peak + jnp.log2(mass)
        kept = stat_cols[...]
        kept = jnp.where(stat_lane == 2 * local, logs, kept)
        stat_cols[...] = jnp.where(stat_lane == 2 * local + 1, delta, kept)
        return g

    def out_copy(ref, i, g):
        return pltpu.make_async_copy(
            stage.at[i, :, group_cols(g)], ref.at[0, :, group_cols(g)], out_sem.at[i, g]
        )

    def forward_group(g, carry):
        receive((0, 1), g)
        send((2, 3), g)
        lax.fori_loop(0, PER, forward_head, g)
        stat_mine[g] = jnp.transpose(stat_cols[...])[:8]
        for side, present in ((0, has_left), (1, has_right)):

            @pl.when(present)
            def _():
                stat_transfer(side, g).start()

        out_copy(att_out, 0, g).start()
        out_copy(dq_out, 1, g).start()
        return carry

    lax.fori_loop(0, GROUPS, forward_group, 0)

    row8 = lax.broadcasted_iota(jnp.int32, (8, HD), 0)
    query_part = jnp.sum(gain_acc[0], axis=0, keepdims=True)
    key_part = jnp.sum(gain_acc[1], axis=0, keepdims=True)
    part[...] = jnp.where(row8 == 0, query_part, jnp.where(row8 == 1, key_part, 0.0))

    def to_ring(i):
        return pltpu.make_async_remote_copy(
            src_ref=part, dst_ref=ring_in.at[i], send_sem=ring_send, recv_sem=ring_recv.at[i],
            device_id={"tm": 0}, device_id_type=MESH,
        )

    @pl.when(has_left)
    def _():
        pl.semaphore_wait(ready, 1)
        to_ring(me).start()

    def backward_head(local, g):
        h = g * PER + local
        at = cols(h)
        kn = kn_own[:, at]
        values = raw[2, :, at]
        dk = acc[0, :, at]
        dv = acc[1, :, at]
        for side in range(2):
            qn = halo[side, 3, :, at]
            grads = halo[side, 2, :, at]
            logs = stat_halo[side, g, pl.ds(2 * local, 1), :]
            delta = stat_halo[side, g, pl.ds(2 * local + 1, 1), :]
            probs = jnp.exp2(dot(kn, qn, NT) * SCALE + bias_b[side] - logs)
            slopes = dot(values, grads, NT)
            change = (probs * (slopes - delta)).astype(jnp.bfloat16)
            dk = dk + dot(change, qn)
            dv = dv + dot(probs.astype(jnp.bfloat16), grads)
        rough = raw[1, :, at].astype(jnp.float32)
        stage[2, :, at] = norm_back(rough, inv_rms(rough), gain_k, dk * ROOT).astype(jnp.bfloat16)
        stage[3, :, at] = dv.astype(jnp.bfloat16)
        return g

    def backward_group(g, carry):
        for side, present in ((0, has_left), (1, has_right)):

            @pl.when(present)
            def _():
                stat_transfer(1 - side, g).wait_recv()

        receive((2, 3), g)
        lax.fori_loop(0, PER, backward_head, g)
        out_copy(dk_out, 2, g).start()
        out_copy(dv_out, 3, g).start()
        return carry

    lax.fori_loop(0, GROUPS, backward_group, 0)

    def to_clip(j, slot):
        return pltpu.make_async_remote_copy(
            src_ref=clip_in.at[clip], dst_ref=clip_in.at[slot], send_sem=clip_send.at[j],
            recv_sem=clip_recv.at[slot], device_id={"clip": lax.rem(clip + j, N_CLIP)},
            device_id_type=MESH,
        )

    def to_all(i):
        return pltpu.make_async_remote_copy(
            src_ref=total, dst_ref=total, send_sem=total_send.at[i], recv_sem=total_recv,
            device_id={"tm": i}, device_id_type=MESH,
        )

    @pl.when(me == 0)
    def _():
        ring = part[...]
        for i in range(1, N_TM):
            to_ring(i).wait_recv()
            ring = ring + ring_in[i]
        clip_in[clip] = ring
        for j in range(1, N_CLIP):
            to_clip(j, clip).start()
        for j in range(1, N_CLIP):
            to_clip(j, lax.rem(clip + j, N_CLIP)).wait_recv()
        everything = clip_in[0]
        for c in range(1, N_CLIP):
            everything = everything + clip_in[c]
        total[...] = everything
        for i in range(1, N_TM):
            to_all(i).start()
        for j in range(1, N_CLIP):
            to_clip(j, clip).wait_send()
        for i in range(1, N_TM):
            to_all(i).wait_send()

    @pl.when(has_left)
    def _():
        to_all(0).wait_recv()
        to_ring(me).wait_send()

    gains_out[...] = total[...]
    for side, present in ((0, has_left), (1, has_right)):

        @pl.when(present)
        def _():
            for g in range(GROUPS):
                for a in range(4):
                    transfer(side, a, g).wait_send()
                stat_transfer(side, g).wait_send()

    for i, ref in enumerate((att_out, dq_out, dk_out, dv_out)):
        for g in range(GROUPS):
            out_copy(ref, i, g).wait()


def finish_kernel(*refs):
    ins, gains, outs, q_total, k_total = refs[:4], refs[4], refs[5:9], refs[9], refs[10]
    held, in_sem, out_sem = refs[11:]
    reads = [pltpu.make_async_copy(ins[i], held.at[i], in_sem.at[i]) for i in range(4)]
    writes = [pltpu.make_async_copy(held.at[i], outs[i], out_sem.at[i]) for i in range(4)]
    for read in reads:
        read.start()
    q_total[...] = gains[0:1]
    k_total[...] = gains[1:2]
    for read, write in zip(reads, writes):
        read.wait()
        write.start()
    for write in writes:
        write.wait()


def on_device(
    queries, key_rows, value_rows, grad_out, query_gain, key_gain, valid_frames, window_start
):
    any_spec = pl.BlockSpec(memory_space=pl.ANY)
    vmem_spec = pl.BlockSpec(memory_space=pltpu.VMEM)
    smem_spec = pl.BlockSpec(memory_space=pltpu.SMEM)
    slab = jax.ShapeDtypeStruct((1, TOK, HH), jnp.bfloat16)
    dma = pltpu.SemaphoreType.DMA
    bf16, f32 = jnp.bfloat16, jnp.float32
    results = pl.pallas_call(
        main_kernel,
        out_shape=[slab] * 4 + [jax.ShapeDtypeStruct((8, HD), f32)],
        in_specs=[any_spec] * 4 + [vmem_spec] * 2 + [smem_spec] * 2,
        out_specs=[any_spec] * 4 + [vmem_spec],
        scratch_shapes=[
            pltpu.VMEM((4, TOK, HH), bf16),
            pltpu.VMEM((2, 4, TOK, HH), bf16),
            pltpu.VMEM((TOK, HH), bf16),
            pltpu.VMEM((TOK, HH), bf16),
            pltpu.VMEM((2, TOK, HH), f32),
            pltpu.VMEM((4, TOK, HH), bf16),
            pltpu.VMEM((3, TOK, TOK), f32),
            pltpu.VMEM((2, TOK, TOK), f32),
            pltpu.VMEM((TOK, HD), f32),
            pltpu.VMEM((GROUPS, 8, TOK), f32),
            pltpu.VMEM((2, GROUPS, 8, TOK), f32),
            pltpu.VMEM((2, 8, HD), f32),
            pltpu.VMEM((8, HD), f32),
            pltpu.VMEM((N_TM, 8, HD), f32),
            pltpu.VMEM((N_CLIP, 8, HD), f32),
            pltpu.VMEM((8, HD), f32),
            dma((4,)),
            dma((4, GROUPS)),
            dma((2, 4, GROUPS)),
            dma((2, 4, GROUPS)),
            dma((2, GROUPS)),
            dma((2, GROUPS)),
            pltpu.SemaphoreType.REGULAR,
            dma,
            dma((N_TM,)),
            dma((N_CLIP,)),
            dma((N_CLIP,)),
            dma((N_TM,)),
            dma,
        ],
        compiler_params=pltpu.CompilerParams(
            collective_id=0, has_side_effects=True, vmem_limit_bytes=58 * 2**20
        ),
        name="attend",
    )(
        queries, key_rows, value_rows, grad_out,
        query_gain.reshape(1, HD), key_gain.reshape(1, HD), valid_frames, window_start,
    )
    row = jax.ShapeDtypeStruct((1, HD), f32)
    outs = pl.pallas_call(
        finish_kernel,
        out_shape=[slab] * 4 + [row] * 2,
        in_specs=[any_spec] * 4 + [vmem_spec],
        out_specs=[any_spec] * 4 + [vmem_spec] * 2,
        scratch_shapes=[pltpu.VMEM((4, 1, TOK, HH), bf16), dma((4,)), dma((4,))],
        compiler_params=pltpu.CompilerParams(vmem_limit_bytes=56 * 2**20),
        name="finish",
    )(*results)
    return (*outs[:4], outs[4].reshape(HD), outs[5].reshape(HD))


def solution(mesh):
    slabs = P("clip", "tm", None)
    return jax.shard_map(
        on_device,
        mesh=mesh,
        in_specs=(slabs,) * 4 + (P(), P(), P("clip", None), P("clip", None)),
        out_specs=(slabs,) * 4 + (P(), P()),
        check_vma=False,
    )
```

profile of v0, /device:TPU:1, one launch (start us, length us, event | category | flops | bytes accessed | tf_op | source)
XLA Modules:
  0.0 61.1 jit_solution(7206698401146471329)
XLA Ops:
  0.6 56.4 %attend.1 = (bf16[1,256,1536]{2,1,0:T(8,128)(2,1)}, bf16[1,256,1536]{2,1,0:T(8,128)(2,1)}, bf16[1,256,1536]{2,1,0:T(8,128)(2,1)}, bf16[1,256,1536]{2,1,0:T(8,128)(2,1)}, f32[8,128]{1,0:T(8,128)}) custom-call(bf16[1,256,1536]{2,1,0:T(8,128)(2,1)} %q_hbm.1, bf16[1,256,1536]{2,1,0:T(8,128)(2,1)} %k_hbm.1, bf16[1,256,1536]{2,1,0:T(8,128)(2,1)} %v_hbm.1, ...), custom_call_target="tpu_custom_call" | custom-call | tf_op jit(solution)/shard_map/attend/pallas_call | solution.py:400
  57.0 4.1 %finish.1 = (bf16[1,256,1536]{2,1,0:T(8,128)(2,1)}, bf16[1,256,1536]{2,1,0:T(8,128)(2,1)}, bf16[1,256,1536]{2,1,0:T(8,128)(2,1)}, bf16[1,256,1536]{2,1,0:T(8,128...) custom-call(bf16[1,256,1536]{2,1,0:T(8,128)(2,1)} %get-tuple-element.17.refs_0_, ...), custom_call_target="tpu_custom_call" | custom-call | tf_op jit(solution)/shard_map/finish/pallas_call | solution.py:445
where the time goes:
time: 61.5 us; the launch traced here: 61.1 us
  Pallas kernels  60.5 us (98%)
  between operations  0.64 us (1%)
    pallas_call x1, Pallas kernels, on_device(): pl.pallas_call(main_kernel, out_shape=[slab] * 4 + [jax.ShapeDtypeStruct(...  56.4 us
    pallas_call x1, Pallas kernels, on_device(): pl.pallas_call(finish_kernel, out_shape=[slab] * 4 + [row] * 2, in_specs=...  4.06 us

commit v1 on v0

--- a/solution.py
+++ b/solution.py
@@ -23,7 +23,8 @@
 ROOT = 1.0 / math.sqrt(HD)
 SCALE = ROOT * math.log2(math.e)
 DEAD = -1e30
-GROUPS = 3
+GROUPS = 6
+AHEAD = 2
 PER = H // GROUPS
 GCOLS = PER * HD
 
@@ -67,8 +68,11 @@
 ):
     me = lax.axis_index("tm")
     clip = lax.axis_index("clip")
-    has_left = me > 0
-    has_right = me < N_TM - 1
+    step = 1 - 2 * lax.rem(me, 2)
+    near = me + step
+    far = me - step
+    has_far = jnp.logical_and(me > 0, me < N_TM - 1)
+    sides = (near, far)
     loads = []
     for i, ref in enumerate((q_hbm, k_hbm, v_hbm, g_hbm)):
         load = pltpu.make_async_copy(ref.at[0], raw.at[i], load_sem.at[i])
@@ -77,13 +81,11 @@
 
     barrier = pltpu.get_barrier_semaphore()
 
-    @pl.when(has_left)
-    def _():
-        pl.semaphore_signal(barrier, inc=1, device_id={"tm": me - 1}, device_id_type=MESH)
-
-    @pl.when(has_right)
-    def _():
-        pl.semaphore_signal(barrier, inc=1, device_id={"tm": me + 1}, device_id_type=MESH)
+    pl.semaphore_signal(barrier, inc=1, device_id={"tm": near}, device_id_type=MESH)
+
+    @pl.when(has_far)
+    def _():
+        pl.semaphore_signal(barrier, inc=1, device_id={"tm": far}, device_id_type=MESH)
 
     @pl.when(me > 1)
     def _():
@@ -99,7 +101,7 @@
         for i in range(1, N_TM):
             pl.semaphore_signal(ready, inc=1, device_id={"tm": i}, device_id_type=MESH)
 
-    @pl.when(jnp.logical_and(has_left, has_right))
+    @pl.when(has_far)
     def _():
         pl.semaphore_wait(barrier, 2)
 
@@ -111,48 +113,51 @@
         source = qn_own if a == 3 else (k_hbm, v_hbm, g_hbm)[a].at[0]
         return pltpu.make_async_remote_copy(
             src_ref=source.at[:, group_cols(g)],
-            dst_ref=halo.at[1 - side, a, :, group_cols(g)],
+            dst_ref=halo.at[side, a, :, group_cols(g)],
             send_sem=send_sem.at[side, a, g],
-            recv_sem=recv_sem.at[1 - side, a, g],
-            device_id={"tm": me + (1 if side else -1)},
+            recv_sem=recv_sem.at[side, a, g],
+            device_id={"tm": sides[side]},
             device_id_type=MESH,
         )
 
     def stat_transfer(side, g):
         return pltpu.make_async_remote_copy(
             src_ref=stat_mine.at[g],
-            dst_ref=stat_halo.at[1 - side, g],
+            dst_ref=stat_halo.at[side, g],
             send_sem=stat_send.at[side, g],
-            recv_sem=stat_recv.at[1 - side, g],
-            device_id={"tm": me + (1 if side else -1)},
+            recv_sem=stat_recv.at[side, g],
+            device_id={"tm": sides[side]},
             device_id_type=MESH,
         )
 
-    def send(arrays, g):
-        for side, present in ((0, has_left), (1, has_right)):
-
-            @pl.when(present)
-            def _():
-                for a in arrays:
-                    transfer(side, a, g).start()
+    def send_near(a):
+        for g in range(GROUPS):
+            transfer(0, a, g).start()
+
+    def send_far(arrays, g):
+        @pl.when(has_far)
+        def _():
+            for a in arrays:
+                transfer(1, a, g).start()
 
     def receive(arrays, g):
-        for side, present in ((0, has_left), (1, has_right)):
-
-            @pl.when(present)
-            def _():
-                for a in arrays:
-                    transfer(1 - side, a, g).wait_recv()
-
-    for g in range(GROUPS):
-        send((0, 1), g)
-
-    for side, present in ((0, has_left), (1, has_right)):
-
-        @pl.when(jnp.logical_not(present))
-        def _():
-            halo[side] = jnp.zeros((4, TOK, HH), jnp.bfloat16)
-            stat_halo[side] = jnp.zeros((GROUPS, 8, TOK), jnp.float32)
+        for a in arrays:
+            transfer(0, a, g).wait_recv()
+
+        @pl.when(has_far)
+        def _():
+            for a in arrays:
+                transfer(1, a, g).wait_recv()
+
+    for g in range(AHEAD):
+        send_far((0, 1), g)
+    for a in (0, 1, 2):
+        send_near(a)
+
+    @pl.when(jnp.logical_not(has_far))
+    def _():
+        halo[1] = jnp.zeros((4, TOK, HH), jnp.bfloat16)
+        stat_halo[1] = jnp.zeros((GROUPS, 8, TOK), jnp.float32)
 
     rows = lax.broadcasted_iota(jnp.int32, (TOK, TOK), 0)
     lanes = lax.broadcasted_iota(jnp.int32, (TOK, TOK), 1)
@@ -170,15 +175,14 @@
         live = (column >= window) & (column < window + WW) & (frame < count)
         return jnp.where(live, 0.0, DEAD).astype(jnp.float32)
 
-    before = jnp.maximum(me - 1, 0)
-    after = jnp.minimum(me + 1, N_TM - 1)
+    known = jnp.where(has_far, far, me)
     mine = window_of(rows, me, me >= 0)
     count_own = frames[0, me]
-    bias_f[0] = bias_of(mine, lanes, jnp.where(has_left, frames[0, before], 0))
+    bias_f[0] = bias_of(mine, lanes, frames[0, near])
     bias_f[1] = bias_of(mine, lanes, count_own)
-    bias_f[2] = bias_of(mine, lanes, jnp.where(has_right, frames[0, after], 0))
-    bias_b[0] = bias_of(window_of(lanes, before, has_left), rows, count_own)
-    bias_b[1] = bias_of(window_of(lanes, after, has_right), rows, count_own)
+    bias_f[2] = bias_of(mine, lanes, jnp.where(has_far, frames[0, known], 0))
+    bias_b[0] = bias_of(window_of(lanes, near, me >= 0), rows, count_own)
+    bias_b[1] = bias_of(window_of(lanes, known, has_far), rows, count_own)
 
     gain_acc[...] = jnp.zeros_like(gain_acc)
     stat_cols[...] = jnp.zeros_like(stat_cols)
@@ -194,6 +198,7 @@
         return carry
 
     lax.fori_loop(0, H, normal_queries, 0)
+    send_near(3)
 
     stat_lane = lax.broadcasted_iota(jnp.int32, (TOK, HD), 1)
 
@@ -249,14 +254,22 @@
 
     def forward_group(g, carry):
         receive((0, 1), g)
-        send((2, 3), g)
-        lax.fori_loop(0, PER, forward_head, g)
+
+        @pl.when(g + AHEAD < GROUPS)
+        def _():
+            send_far((0, 1), g + AHEAD)
+
+        @pl.when(g + AHEAD >= GROUPS)
+        def _():
+            send_far((2, 3), g + AHEAD - GROUPS)
+
+        lax.fori_loop(0, PER, forward_head, g, unroll=True)
         stat_mine[g] = jnp.transpose(stat_cols[...])[:8]
-        for side, present in ((0, has_left), (1, has_right)):
-
-            @pl.when(present)
-            def _():
-                stat_transfer(side, g).start()
+        stat_transfer(0, g).start()
+
+        @pl.when(has_far)
+        def _():
+            stat_transfer(1, g).start()
 
         out_copy(att_out, 0, g).start()
         out_copy(dq_out, 1, g).start()
@@ -275,10 +288,43 @@
             device_id={"tm": 0}, device_id_type=MESH,
         )
 
-    @pl.when(has_left)
+    @pl.when(me > 0)
     def _():
         pl.semaphore_wait(ready, 1)
         to_ring(me).start()
+
+    def to_clip(j, slot):
+        return pltpu.make_async_remote_copy(
+            src_ref=clip_in.at[clip], dst_ref=clip_in.at[slot], send_sem=clip_send.at[j],
+            recv_sem=clip_recv.at[slot], device_id={"clip": lax.rem(clip + j, N_CLIP)},
+            device_id_type=MESH,
+        )
+
+    def to_all(i):
+        return pltpu.make_async_remote_copy(
+            src_ref=total, dst_ref=total, send_sem=total_send.at[i], recv_sem=total_recv,
+            device_id={"tm": i}, device_id_type=MESH,
+        )
+
+    @pl.when(me == 0)
+    def _():
+        ring = part[...]
+        for i in range(1, N_TM):
+            to_ring(i).wait_recv()
+            ring = ring + ring_in[i]
+        clip_in[clip] = ring
+        for j in range(1, N_CLIP):
+            to_clip(j, clip).start()
+
+    def share_total():
+        for j in range(1, N_CLIP):
+            to_clip(j, lax.rem(clip + j, N_CLIP)).wait_recv()
+        everything = clip_in[0]
+        for c in range(1, N_CLIP):
+            everything = everything + clip_in[c]
+        total[...] = everything
+        for i in range(1, N_TM):
+            to_all(i).start()
 
     def backward_head(local, g):
         h = g * PER + local
@@ -303,69 +349,54 @@
         return g
 
     def backward_group(g, carry):
-        for side, present in ((0, has_left), (1, has_right)):
-
-            @pl.when(present)
-            def _():
-                stat_transfer(1 - side, g).wait_recv()
+        stat_transfer(0, g).wait_recv()
+
+        @pl.when(has_far)
+        def _():
+            stat_transfer(1, g).wait_recv()
 
         receive((2, 3), g)
-        lax.fori_loop(0, PER, backward_head, g)
+
+        @pl.when(g + AHEAD < GROUPS)
+        def _():
+            send_far((2, 3), g + AHEAD)
+
+        lax.fori_loop(0, PER, backward_head, g, unroll=True)
         out_copy(dk_out, 2, g).start()
         out_copy(dv_out, 3, g).start()
         return carry
 
     lax.fori_loop(0, GROUPS, backward_group, 0)
 
-    def to_clip(j, slot):
-        return pltpu.make_async_remote_copy(
-            src_ref=clip_in.at[clip], dst_ref=clip_in.at[slot], send_sem=clip_send.at[j],
-            recv_sem=clip_recv.at[slot], device_id={"clip": lax.rem(clip + j, N_CLIP)},
-            device_id_type=MESH,
-        )
-
-    def to_all(i):
-        return pltpu.make_async_remote_copy(
-            src_ref=total, dst_ref=total, send_sem=total_send.at[i], recv_sem=total_recv,
-            device_id={"tm": i}, device_id_type=MESH,
-        )
-
     @pl.when(me == 0)
     def _():
-        ring = part[...]
-        for i in range(1, N_TM):
-            to_ring(i).wait_recv()
-            ring = ring + ring_in[i]
-        clip_in[clip] = ring
-        for j in range(1, N_CLIP):
-            to_clip(j, clip).start()
-        for j in range(1, N_CLIP):
-            to_clip(j, lax.rem(clip + j, N_CLIP)).wait_recv()
-        everything = clip_in[0]
-        for c in range(1, N_CLIP):
-            everything = everything + clip_in[c]
-        total[...] = everything
-        for i in range(1, N_TM):
-            to_all(i).start()
+        share_total()
+
+
+    @pl.when(me > 0)
+    def _():
+        to_all(0).wait_recv()
+        to_ring(me).wait_send()
+
+    @pl.when(me == 0)
+    def _():
         for j in range(1, N_CLIP):
             to_clip(j, clip).wait_send()
         for i in range(1, N_TM):
             to_all(i).wait_send()
 
-    @pl.when(has_left)
-    def _():
-        to_all(0).wait_recv()
-        to_ring(me).wait_send()
-
     gains_out[...] = total[...]
-    for side, present in ((0, has_left), (1, has_right)):
-
-        @pl.when(present)
-        def _():
-            for g in range(GROUPS):
-                for a in range(4):
-                    transfer(side, a, g).wait_send()
-                stat_transfer(side, g).wait_send()
+    def all_sent(side):
+        for g in range(GROUPS):
+            for a in range(4):
+                transfer(side, a, g).wait_send()
+            stat_transfer(side, g).wait_send()
+
+    all_sent(0)
+
+    @pl.when(has_far)
+    def _():
+        all_sent(1)
 
     for i, ref in enumerate((att_out, dq_out, dk_out, dv_out)):
         for g in range(GROUPS):
@@ -374,16 +405,12 @@
 
 def finish_kernel(*refs):
     ins, gains, outs, q_total, k_total = refs[:4], refs[4], refs[5:9], refs[9], refs[10]
-    held, in_sem, out_sem = refs[11:]
-    reads = [pltpu.make_async_copy(ins[i], held.at[i], in_sem.at[i]) for i in range(4)]
-    writes = [pltpu.make_async_copy(held.at[i], outs[i], out_sem.at[i]) for i in range(4)]
-    for read in reads:
-        read.start()
+    out_sem = refs[11]
+    writes = [pltpu.make_async_copy(ins[i], outs[i], out_sem.at[i]) for i in range(4)]
+    for write in writes:
+        write.start()
     q_total[...] = gains[0:1]
     k_total[...] = gains[1:2]
-    for read, write in zip(reads, writes):
-        read.wait()
-        write.start()
     for write in writes:
         write.wait()
 
@@ -434,7 +461,7 @@
             dma,
         ],
         compiler_params=pltpu.CompilerParams(
-            collective_id=0, has_side_effects=True, vmem_limit_bytes=58 * 2**20
+            collective_id=0, has_side_effects=True, vmem_limit_bytes=203 * 2**18
         ),
         name="attend",
     )(
@@ -445,10 +472,10 @@
     outs = pl.pallas_call(
         finish_kernel,
         out_shape=[slab] * 4 + [row] * 2,
-        in_specs=[any_spec] * 4 + [vmem_spec],
+        in_specs=[vmem_spec] * 5,
         out_specs=[any_spec] * 4 + [vmem_spec] * 2,
-        scratch_shapes=[pltpu.VMEM((4, 1, TOK, HH), bf16), dma((4,)), dma((4,))],
-        compiler_params=pltpu.CompilerParams(vmem_limit_bytes=56 * 2**20),
+        scratch_shapes=[dma((4,))],
+        compiler_params=pltpu.CompilerParams(vmem_limit_bytes=8 * 2**20),
         name="finish",
     )(*results)
     return (*outs[:4], outs[4].reshape(HD), outs[5].reshape(HD))

time: 61.5 us -> 51.5 us (0.84)
  Pallas kernels: 60.5 us -> 50 us
  local copies, waits for them, and re-layouts: 0 us -> 0.67 us
    pallas_call x1, Pallas kernels: 56.4 us -> 47.8 us  [on_device(): pl.pallas_call(main_kernel, out_shape=[slab] * 4 + [jax.ShapeDtypeStruct(...]
    pallas_call x1, Pallas kernels: 4.06 us -> 2.21 us  [on_device(): pl.pallas_call(finish_kernel, out_shape=[slab] * 4 + [row] * 2, in_specs=...]
    unnamed x0 -> x8, local copies, waits for them, and re-layouts: none -> 0.67 us
where the time goes in v1:
time: 51.5 us; the launch traced here: 51.4 us
  Pallas kernels  50 us (97%)
  between operations  0.68 us (1%)
  local copies, waits for them, and re-layouts  0.67 us (1%)
    pallas_call x1, Pallas kernels, on_device(): pl.pallas_call(main_kernel, out_shape=[slab] * 4 + [jax.ShapeDtypeStruct(...  47.8 us
    pallas_call x1, Pallas kernels, on_device(): pl.pallas_call(finish_kernel, out_shape=[slab] * 4 + [row] * 2, in_specs=...  2.21 us

profile of v1, /device:TPU:1, one launch (start us, length us, event | category | flops | bytes accessed | tf_op | source)
XLA Modules:
  0.0 51.4 jit_solution(10848100446373100298)
XLA Ops:
  0.6 0.0 copy-start.3
  0.6 0.0 copy-start
  0.7 0.0 copy-start.1
  0.7 0.0 copy-start.2
  0.7 0.6 %copy-done.3 = s32[1,64]{1,0:T(1,128)S(1)} copy-done((s32[1,64]{1,0:T(1,128)S(1)}, s32[1,64]{1,0:T(1,128)}, u32[]{:S(2)}) %copy-start.3) | copy-done | bytes 280
  1.3 0.0 copy-done
  1.3 0.0 copy-done.1
  1.3 0.0 copy-done.2
  1.3 47.8 %attend.1 = (bf16[1,256,1536]{2,1,0:T(8,128)(2,1)S(1)}, bf16[1,256,1536]{2,1,0:T(8,128)(2,1)S(1)}, bf16[1,256,1536]{2,1,0:T(8,128)(2,1)S(1)}, bf16[1,256,1536]{2,1,0:T(8,128)(2,1)S(1)}, f32[8,128]{1,0:T(8,128)S(1)}) custom-call(bf16[1,256,1536]{2,1,0:T(8,128)(2,1)} %q_hbm.1, bf16[1,256,1536]{2,1,0:T(8,128)(2,1)} %k_hbm.1, bf16[1,256,1536]{2,1,0:T(8,128)(2,1)} %v_hbm.1, ...), custom_call_target="tpu_custom_call" | custom-call | tf_op jit(solution)/shard_map/attend/pallas_call | solution.py:427
  49.2 2.2 %finish.1 = (bf16[1,256,1536]{2,1,0:T(8,128)(2,1)}, bf16[1,256,1536]{2,1,0:T(8,128)(2,1)}, bf16[1,256,1536]{2,1,0:T(8,128)(2,1)}, bf16[1,256,1536]{2,1,0:T(8,128...) custom-call(bf16[1,256,1536]{2,1,0:T(8,128)(2,1)S(1)} %get-tuple-element.17.refs_0_, ...), custom_call_target="tpu_custom_call" | custom-call | tf_op jit(solution)/shard_map/finish/pallas_call | solution.py:472
Async XLA Ops:
  0.6 0.7 %copy-start.3 = (s32[1,64]{1,0:T(1,128)S(1)}, s32[1,64]{1,0:T(1,128)}, u32[]{:S(2)}) copy-start(s32[1,64]{1,0:T(1,128)} %starts.1) | copy-start | bytes 772
  0.6 0.7 %copy-start = (f32[128]{0:T(128)S(1)}, f32[128]{0:T(128)}, u32[]{:S(2)}) copy-start(f32[128]{0:T(128)} %param.12) | copy-start | bytes 1540
  0.7 0.7 %copy-start.1 = (f32[128]{0:T(128)S(1)}, f32[128]{0:T(128)}, u32[]{:S(2)}) copy-start(f32[128]{0:T(128)} %param.13) | copy-start | bytes 1540
  0.7 0.7 %copy-start.2 = (s32[1,16]{1,0:T(1,128)S(1)}, s32[1,16]{1,0:T(1,128)}, u32[]{:S(2)}) copy-start(s32[1,16]{1,0:T(1,128)} %frames.1) | copy-start | bytes 196

commit v2 on v1

--- a/solution.py
+++ b/solution.py
@@ -24,9 +24,9 @@
 SCALE = ROOT * math.log2(math.e)
 DEAD = -1e30
 GROUPS = 6
-AHEAD = 2
 PER = H // GROUPS
-GCOLS = PER * HD
+FULL = GROUPS - 1
+PACKETS = FULL + PER
 
 NT = (((1,), (1,)), ((), ()))
 TN = (((0,), (0,)), ((), ()))
@@ -40,8 +40,11 @@
     return pl.ds(pl.multiple_of(h * HD, HD), HD)
 
 
-def group_cols(g):
-    return pl.ds(pl.multiple_of(g * GCOLS, GCOLS), GCOLS)
+def packet_cols(n):
+    if isinstance(n, int):
+        first, count = (n * PER, PER) if n < FULL else (FULL * PER + n - FULL, 1)
+        return pl.ds(first * HD, count * HD)
+    return pl.ds(pl.multiple_of(n * PER * HD, PER * HD), PER * HD)
 
 
 def inv_rms(values):
@@ -59,11 +62,11 @@
 
 
 def main_kernel(
-    q_hbm, k_hbm, v_hbm, g_hbm, q_gain, k_gain, frames, starts,
+    q_hbm, k_hbm, v_hbm, g_hbm, q_gain_any, k_gain_any, frames_any, starts_any,
     att_out, dq_out, dk_out, dv_out, gains_out,
-    raw, halo, qn_own, kn_own, acc, stage, bias_f, bias_b,
+    q_gain, k_gain, frames, starts, raw, halo, qn_own, kn_own, acc, stage, bias_f, bias_b,
     stat_cols, stat_mine, stat_halo, gain_acc, part, ring_in, clip_in, total,
-    load_sem, out_sem, send_sem, recv_sem, stat_send, stat_recv,
+    small_sem, load_sem, out_sem, send_sem, recv_sem, stat_send, stat_recv,
     ready, ring_send, ring_recv, clip_send, clip_recv, total_send, total_recv,
 ):
     me = lax.axis_index("tm")
@@ -73,11 +76,19 @@
     far = me - step
     has_far = jnp.logical_and(me > 0, me < N_TM - 1)
     sides = (near, far)
+    middle = jnp.logical_or(me == N_TM // 2 - 1, me == N_TM // 2)
     loads = []
     for i, ref in enumerate((q_hbm, k_hbm, v_hbm, g_hbm)):
         load = pltpu.make_async_copy(ref.at[0], raw.at[i], load_sem.at[i])
         load.start()
         loads.append(load)
+
+    small = []
+    pairs = ((q_gain_any, q_gain), (k_gain_any, k_gain), (frames_any, frames), (starts_any, starts))
+    for i, (source, target) in enumerate(pairs):
+        load = pltpu.make_async_copy(source, target, small_sem.at[i])
+        load.start()
+        small.append(load)
 
     barrier = pltpu.get_barrier_semaphore()
 
@@ -112,8 +123,8 @@
     def transfer(side, a, g):
         source = qn_own if a == 3 else (k_hbm, v_hbm, g_hbm)[a].at[0]
         return pltpu.make_async_remote_copy(
-            src_ref=source.at[:, group_cols(g)],
-            dst_ref=halo.at[side, a, :, group_cols(g)],
+            src_ref=source.at[:, packet_cols(g)],
+            dst_ref=halo.at[side, a, :, packet_cols(g)],
             send_sem=send_sem.at[side, a, g],
             recv_sem=recv_sem.at[side, a, g],
             device_id={"tm": sides[side]},
@@ -131,7 +142,7 @@
         )
 
     def send_near(a):
-        for g in range(GROUPS):
+        for g in range(PACKETS):
             transfer(0, a, g).start()
 
     def send_far(arrays, g):
@@ -140,16 +151,17 @@
             for a in arrays:
                 transfer(1, a, g).start()
 
-    def receive(arrays, g):
+    def receive_near(arrays, g):
         for a in arrays:
             transfer(0, a, g).wait_recv()
 
+    def receive_far(arrays, g):
         @pl.when(has_far)
         def _():
             for a in arrays:
                 transfer(1, a, g).wait_recv()
 
-    for g in range(AHEAD):
+    for g in range(PACKETS):
         send_far((0, 1), g)
     for a in (0, 1, 2):
         send_near(a)
@@ -159,6 +171,8 @@
         halo[1] = jnp.zeros((4, TOK, HH), jnp.bfloat16)
         stat_halo[1] = jnp.zeros((GROUPS, 8, TOK), jnp.float32)
 
+    for load in small:
+        load.wait()
     rows = lax.broadcasted_iota(jnp.int32, (TOK, TOK), 0)
     lanes = lax.broadcasted_iota(jnp.int32, (TOK, TOK), 1)
 
@@ -198,6 +212,12 @@
         return carry
 
     lax.fori_loop(0, H, normal_queries, 0)
+    send_far((2, 3), 0)
+
+    @pl.when(middle)
+    def _():
+        send_far((2, 3), 1)
+
     send_near(3)
 
     stat_lane = lax.broadcasted_iota(jnp.int32, (TOK, HD), 1)
@@ -249,21 +269,10 @@
 
     def out_copy(ref, i, g):
         return pltpu.make_async_copy(
-            stage.at[i, :, group_cols(g)], ref.at[0, :, group_cols(g)], out_sem.at[i, g]
-        )
-
-    def forward_group(g, carry):
-        receive((0, 1), g)
-
-        @pl.when(g + AHEAD < GROUPS)
-        def _():
-            send_far((0, 1), g + AHEAD)
-
-        @pl.when(g + AHEAD >= GROUPS)
-        def _():
-            send_far((2, 3), g + AHEAD - GROUPS)
-
-        lax.fori_loop(0, PER, forward_head, g, unroll=True)
+            stage.at[i, :, packet_cols(g)], ref.at[0, :, packet_cols(g)], out_sem.at[i, g]
+        )
+
+    def keep_stats(g):
         stat_mine[g] = jnp.transpose(stat_cols[...])[:8]
         stat_transfer(0, g).start()
 
@@ -271,11 +280,20 @@
         def _():
             stat_transfer(1, g).start()
 
+    def forward_group(g, carry):
+        receive_near((0, 1), g)
+        receive_far((0, 1), g)
+        lax.fori_loop(0, PER, forward_head, g, unroll=True)
+        keep_stats(g)
         out_copy(att_out, 0, g).start()
         out_copy(dq_out, 1, g).start()
         return carry
 
-    lax.fori_loop(0, GROUPS, forward_group, 0)
+    lax.fori_loop(0, FULL, forward_group, 0)
+    for local in range(PER):
+        receive_near((0, 1), FULL + local)
+        receive_far((0, 1), FULL + local)
+        forward_head(local, FULL)
 
     row8 = lax.broadcasted_iota(jnp.int32, (8, HD), 0)
     query_part = jnp.sum(gain_acc[0], axis=0, keepdims=True)
@@ -292,6 +310,19 @@
     def _():
         pl.semaphore_wait(ready, 1)
         to_ring(me).start()
+
+    keep_stats(FULL)
+
+    @pl.when(jnp.logical_not(middle))
+    def _():
+        send_far((2, 3), 1)
+
+    for g in range(2, PACKETS):
+        send_far((2, 3), g)
+
+    for n in range(FULL, PACKETS):
+        out_copy(att_out, 0, n).start()
+        out_copy(dq_out, 1, n).start()
 
     def to_clip(j, slot):
         return pltpu.make_async_remote_copy(
@@ -326,23 +357,30 @@
         for i in range(1, N_TM):
             to_all(i).start()
 
-    def backward_head(local, g):
-        h = g * PER + local
-        at = cols(h)
-        kn = kn_own[:, at]
-        values = raw[2, :, at]
-        dk = acc[0, :, at]
-        dv = acc[1, :, at]
-        for side in range(2):
-            qn = halo[side, 3, :, at]
-            grads = halo[side, 2, :, at]
-            logs = stat_halo[side, g, pl.ds(2 * local, 1), :]
-            delta = stat_halo[side, g, pl.ds(2 * local + 1, 1), :]
-            probs = jnp.exp2(dot(kn, qn, NT) * SCALE + bias_b[side] - logs)
-            slopes = dot(values, grads, NT)
-            change = (probs * (slopes - delta)).astype(jnp.bfloat16)
-            dk = dk + dot(change, qn)
-            dv = dv + dot(probs.astype(jnp.bfloat16), grads)
+    def backward_terms(side, local, g):
+        at = cols(g * PER + local)
+        qn = halo[side, 3, :, at]
+        grads = halo[side, 2, :, at]
+        logs = stat_halo[side, g, pl.ds(2 * local, 1), :]
+        delta = stat_halo[side, g, pl.ds(2 * local + 1, 1), :]
+        probs = jnp.exp2(dot(kn_own[:, at], qn, NT) * SCALE + bias_b[side] - logs)
+        slopes = dot(raw[2, :, at], grads, NT)
+        change = (probs * (slopes - delta)).astype(jnp.bfloat16)
+        return (
+            acc[0, :, at] + dot(change, qn),
+            acc[1, :, at] + dot(probs.astype(jnp.bfloat16), grads),
+        )
+
+    def near_head(local, g):
+        at = cols(g * PER + local)
+        dk, dv = backward_terms(0, local, g)
+        acc[0, :, at] = dk
+        acc[1, :, at] = dv
+        return g
+
+    def far_head(local, g):
+        at = cols(g * PER + local)
+        dk, dv = backward_terms(1, local, g)
         rough = raw[1, :, at].astype(jnp.float32)
         stage[2, :, at] = norm_back(rough, inv_rms(rough), gain_k, dk * ROOT).astype(jnp.bfloat16)
         stage[3, :, at] = dv.astype(jnp.bfloat16)
@@ -350,23 +388,35 @@
 
     def backward_group(g, carry):
         stat_transfer(0, g).wait_recv()
+        receive_near((2, 3), g)
+        lax.fori_loop(0, PER, near_head, g, unroll=True)
 
         @pl.when(has_far)
         def _():
             stat_transfer(1, g).wait_recv()
 
-        receive((2, 3), g)
-
-        @pl.when(g + AHEAD < GROUPS)
-        def _():
-            send_far((2, 3), g + AHEAD)
-
-        lax.fori_loop(0, PER, backward_head, g, unroll=True)
+        receive_far((2, 3), g)
+
+        lax.fori_loop(0, PER, far_head, g, unroll=True)
         out_copy(dk_out, 2, g).start()
         out_copy(dv_out, 3, g).start()
         return carry
 
-    lax.fori_loop(0, GROUPS, backward_group, 0)
+    lax.fori_loop(0, FULL, backward_group, 0)
+    stat_transfer(0, FULL).wait_recv()
+    for local in range(PER):
+        receive_near((2, 3), FULL + local)
+        near_head(local, FULL)
+
+    @pl.when(has_far)
+    def _():
+        stat_transfer(1, FULL).wait_recv()
+
+    for local in range(PER):
+        receive_far((2, 3), FULL + local)
+        far_head(local, FULL)
+        out_copy(dk_out, 2, FULL + local).start()
+        out_copy(dv_out, 3, FULL + local).start()
 
     @pl.when(me == 0)
     def _():
@@ -387,9 +437,10 @@
 
     gains_out[...] = total[...]
     def all_sent(side):
+        for n in range(PACKETS):
+            for a in range(4):
+                transfer(side, a, n).wait_send()
         for g in range(GROUPS):
-            for a in range(4):
-                transfer(side, a, g).wait_send()
             stat_transfer(side, g).wait_send()
 
     all_sent(0)
@@ -399,8 +450,8 @@
         all_sent(1)
 
     for i, ref in enumerate((att_out, dq_out, dk_out, dv_out)):
-        for g in range(GROUPS):
-            out_copy(ref, i, g).wait()
+        for n in range(PACKETS):
+            out_copy(ref, i, n).wait()
 
 
 def finish_kernel(*refs):
@@ -420,16 +471,19 @@
 ):
     any_spec = pl.BlockSpec(memory_space=pl.ANY)
     vmem_spec = pl.BlockSpec(memory_space=pltpu.VMEM)
-    smem_spec = pl.BlockSpec(memory_space=pltpu.SMEM)
     slab = jax.ShapeDtypeStruct((1, TOK, HH), jnp.bfloat16)
     dma = pltpu.SemaphoreType.DMA
     bf16, f32 = jnp.bfloat16, jnp.float32
     results = pl.pallas_call(
         main_kernel,
         out_shape=[slab] * 4 + [jax.ShapeDtypeStruct((8, HD), f32)],
-        in_specs=[any_spec] * 4 + [vmem_spec] * 2 + [smem_spec] * 2,
+        in_specs=[any_spec] * 8,
         out_specs=[any_spec] * 4 + [vmem_spec],
         scratch_shapes=[
+            pltpu.VMEM((1, HD), f32),
+            pltpu.VMEM((1, HD), f32),
+            pltpu.SMEM((1, N_TM), jnp.int32),
+            pltpu.SMEM((1, N_TM * GW), jnp.int32),
             pltpu.VMEM((4, TOK, HH), bf16),
             pltpu.VMEM((2, 4, TOK, HH), bf16),
             pltpu.VMEM((TOK, HH), bf16),
@@ -447,9 +501,10 @@
             pltpu.VMEM((N_CLIP, 8, HD), f32),
             pltpu.VMEM((8, HD), f32),
             dma((4,)),
-            dma((4, GROUPS)),
-            dma((2, 4, GROUPS)),
-            dma((2, 4, GROUPS)),
+            dma((4,)),
+            dma((4, PACKETS)),
+            dma((2, 4, PACKETS)),
+            dma((2, 4, PACKETS)),
             dma((2, GROUPS)),
             dma((2, GROUPS)),
             pltpu.SemaphoreType.REGULAR,

time: 51.5 us -> 48.7 us (0.946)
  Pallas kernels: 50 us -> 47 us
    pallas_call x1, Pallas kernels: 47.8 us -> 44.8 us  [on_device(): pl.pallas_call(main_kernel, out_shape=[slab] * 4 + [jax.ShapeDtypeStruct(...]
where the time goes in v2:
time: 48.7 us; the launch traced here: 48.3 us
  Pallas kernels  47 us (97%)
  between operations  0.68 us (1%)
  local copies, waits for them, and re-layouts  0.67 us (1%)
    pallas_call x1, Pallas kernels, on_device(): pl.pallas_call(main_kernel, out_shape=[slab] * 4 + [jax.ShapeDtypeStruct(...  44.8 us
    pallas_call x1, Pallas kernels, on_device(): pl.pallas_call(finish_kernel, out_shape=[slab] * 4 + [row] * 2, in_specs=...  2.21 us

profile of v2, /device:TPU:1, one launch (start us, length us, event | category | flops | bytes accessed | tf_op | source)
XLA Modules:
  0.0 48.3 jit_solution(8043257577711762210)
XLA Ops:
  0.6 0.0 copy-start.3
  0.6 0.0 copy-start
  0.7 0.0 copy-start.1
  0.7 0.0 copy-start.2
  0.7 0.6 %copy-done.3 = s32[1,64]{1,0:T(1,128)S(1)} copy-done((s32[1,64]{1,0:T(1,128)S(1)}, s32[1,64]{1,0:T(1,128)}, u32[]{:S(2)}) %copy-start.3) | copy-done | bytes 280
  1.3 0.0 copy-done
  1.3 0.0 copy-done.1
  1.3 0.0 copy-done.2
  1.3 44.8 %attend.1 = (bf16[1,256,1536]{2,1,0:T(8,128)(2,1)S(1)}, bf16[1,256,1536]{2,1,0:T(8,128)(2,1)S(1)}, bf16[1,256,1536]{2,1,0:T(8,128)(2,1)S(1)}, bf16[1,256,1536]{2,1,0:T(8,128)(2,1)S(1)}, f32[8,128]{1,0:T(8,128)S(1)}) custom-call(bf16[1,256,1536]{2,1,0:T(8,128)(2,1)} %q_hbm.1, bf16[1,256,1536]{2,1,0:T(8,128)(2,1)} %k_hbm.1, bf16[1,256,1536]{2,1,0:T(8,128)(2,1)} %v_hbm.1, ...), custom_call_target="tpu_custom_call" | custom-call | tf_op jit(solution)/shard_map/attend/pallas_call | solution.py:477
  46.1 2.2 %finish.1 = (bf16[1,256,1536]{2,1,0:T(8,128)(2,1)}, bf16[1,256,1536]{2,1,0:T(8,128)(2,1)}, bf16[1,256,1536]{2,1,0:T(8,128)(2,1)}, bf16[1,256,1536]{2,1,0:T(8,128...) custom-call(bf16[1,256,1536]{2,1,0:T(8,128)(2,1)S(1)} %get-tuple-element.17.refs_0_, ...), custom_call_target="tpu_custom_call" | custom-call | tf_op jit(solution)/shard_map/finish/pallas_call | solution.py:527
Async XLA Ops:
  0.6 0.7 %copy-start.3 = (s32[1,64]{1,0:T(1,128)S(1)}, s32[1,64]{1,0:T(1,128)}, u32[]{:S(2)}) copy-start(s32[1,64]{1,0:T(1,128)} %starts_any.1) | copy-start | bytes 772
  0.6 0.7 %copy-start = (f32[128]{0:T(128)S(1)}, f32[128]{0:T(128)}, u32[]{:S(2)}) copy-start(f32[128]{0:T(128)} %param.12) | copy-start | bytes 1540
  0.7 0.7 %copy-start.1 = (f32[128]{0:T(128)S(1)}, f32[128]{0:T(128)}, u32[]{:S(2)}) copy-start(f32[128]{0:T(128)} %param.13) | copy-start | bytes 1540
  0.7 0.7 %copy-start.2 = (s32[1,16]{1,0:T(1,128)S(1)}, s32[1,16]{1,0:T(1,128)}, u32[]{:S(2)}) copy-start(s32[1,16]{1,0:T(1,128)} %frames_any.1) | copy-start | bytes 196

commit v3 on v2

--- a/solution.py
+++ b/solution.py
@@ -77,6 +77,18 @@
     has_far = jnp.logical_and(me > 0, me < N_TM - 1)
     sides = (near, far)
     middle = jnp.logical_or(me == N_TM // 2 - 1, me == N_TM // 2)
+    barrier = pltpu.get_barrier_semaphore()
+
+    pl.semaphore_signal(barrier, inc=1, device_id={"tm": near}, device_id_type=MESH)
+
+    @pl.when(has_far)
+    def _():
+        pl.semaphore_signal(barrier, inc=1, device_id={"tm": far}, device_id_type=MESH)
+
+    @pl.when(me > 1)
+    def _():
+        pl.semaphore_signal(barrier, inc=1, device_id={"tm": 0}, device_id_type=MESH)
+
     loads = []
     for i, ref in enumerate((q_hbm, k_hbm, v_hbm, g_hbm)):
         load = pltpu.make_async_copy(ref.at[0], raw.at[i], load_sem.at[i])
@@ -89,18 +101,6 @@
         load = pltpu.make_async_copy(source, target, small_sem.at[i])
         load.start()
         small.append(load)
-
-    barrier = pltpu.get_barrier_semaphore()
-
-    pl.semaphore_signal(barrier, inc=1, device_id={"tm": near}, device_id_type=MESH)
-
-    @pl.when(has_far)
-    def _():
-        pl.semaphore_signal(barrier, inc=1, device_id={"tm": far}, device_id_type=MESH)
-
-    @pl.when(me > 1)
-    def _():
-        pl.semaphore_signal(barrier, inc=1, device_id={"tm": 0}, device_id_type=MESH)
 
     @pl.when(me == 0)
     def _():
@@ -216,7 +216,7 @@
 
     @pl.when(middle)
     def _():
-        send_far((2, 3), 1)
+        send_far((2,), 1)
 
     send_near(3)
 
@@ -315,7 +315,9 @@
 
     @pl.when(jnp.logical_not(middle))
     def _():
-        send_far((2, 3), 1)
+        send_far((2,), 1)
+
+    send_far((3,), 1)
 
     for g in range(2, PACKETS):
         send_far((2, 3), g)
@@ -324,10 +326,10 @@
         out_copy(att_out, 0, n).start()
         out_copy(dq_out, 1, n).start()
 
-    def to_clip(j, slot):
+    def to_clip(c, slot):
         return pltpu.make_async_remote_copy(
-            src_ref=clip_in.at[clip], dst_ref=clip_in.at[slot], send_sem=clip_send.at[j],
-            recv_sem=clip_recv.at[slot], device_id={"clip": lax.rem(clip + j, N_CLIP)},
+            src_ref=clip_in.at[clip], dst_ref=clip_in.at[slot], send_sem=clip_send.at[c],
+            recv_sem=clip_recv.at[slot], device_id={"clip": c},
             device_id_type=MESH,
         )
 
@@ -344,12 +346,19 @@
             to_ring(i).wait_recv()
             ring = ring + ring_in[i]
         clip_in[clip] = ring
-        for j in range(1, N_CLIP):
-            to_clip(j, clip).start()
+        for c in range(N_CLIP):
+
+            @pl.when(clip != c)
+            def _():
+                to_clip(c, clip).start()
 
     def share_total():
-        for j in range(1, N_CLIP):
-            to_clip(j, lax.rem(clip + j, N_CLIP)).wait_recv()
+        for c in range(N_CLIP):
+
+            @pl.when(clip != c)
+            def _():
+                to_clip(c, c).wait_recv()
+
         everything = clip_in[0]
         for c in range(1, N_CLIP):
             everything = everything + clip_in[c]
@@ -408,9 +417,32 @@
         receive_near((2, 3), FULL + local)
         near_head(local, FULL)
 
+    def all_sent(side, arrays):
+        for n in range(PACKETS):
+            for a in arrays:
+                transfer(side, a, n).wait_send()
+
+    all_sent(0, (0, 1, 2, 3))
+    for g in range(GROUPS):
+        stat_transfer(0, g).wait_send()
+
     @pl.when(has_far)
     def _():
+        all_sent(1, (0, 1))
+        for g in range(GROUPS):
+            stat_transfer(1, g).wait_send()
         stat_transfer(1, FULL).wait_recv()
+
+    @pl.when(me > 0)
+    def _():
+        to_ring(me).wait_send()
+
+    for n in range(PACKETS):
+        out_copy(att_out, 0, n).wait()
+        out_copy(dq_out, 1, n).wait()
+    for n in range(FULL):
+        out_copy(dk_out, 2, n).wait()
+        out_copy(dv_out, 3, n).wait()
 
     for local in range(PER):
         receive_far((2, 3), FULL + local)
@@ -422,36 +454,30 @@
     def _():
         share_total()
 
-
-    @pl.when(me > 0)
-    def _():
-        to_all(0).wait_recv()
-        to_ring(me).wait_send()
+    @pl.when(has_far)
+    def _():
+        all_sent(1, (2, 3))
+
+    for n in range(FULL, PACKETS):
+        out_copy(dk_out, 2, n).wait()
+        out_copy(dv_out, 3, n).wait()
 
     @pl.when(me == 0)
     def _():
-        for j in range(1, N_CLIP):
-            to_clip(j, clip).wait_send()
+        for c in range(N_CLIP):
+
+            @pl.when(clip != c)
+            def _():
+                to_clip(c, clip).wait_send()
+
         for i in range(1, N_TM):
             to_all(i).wait_send()
 
+    @pl.when(me > 0)
+    def _():
+        to_all(0).wait_recv()
+
     gains_out[...] = total[...]
-    def all_sent(side):
-        for n in range(PACKETS):
-            for a in range(4):
-                transfer(side, a, n).wait_send()
-        for g in range(GROUPS):
-            stat_transfer(side, g).wait_send()
-
-    all_sent(0)
-
-    @pl.when(has_far)
-    def _():
-        all_sent(1)
-
-    for i, ref in enumerate((att_out, dq_out, dk_out, dv_out)):
-        for n in range(PACKETS):
-            out_copy(ref, i, n).wait()
 
 
 def finish_kernel(*refs):

time: 48.7 us -> 46.9 us (0.963)
  Pallas kernels: 47 us -> 45.3 us
    pallas_call x1, Pallas kernels: 44.8 us -> 43.1 us  [on_device(): pl.pallas_call(main_kernel, out_shape=[slab] * 4 + [jax.ShapeDtypeStruct(...]
where the time goes in v3:
time: 46.9 us; the launch traced here: 46.7 us
  Pallas kernels  45.3 us (97%)
  between operations  0.68 us (1%)
  local copies, waits for them, and re-layouts  0.67 us (1%)
    pallas_call x1, Pallas kernels, on_device(): pl.pallas_call(main_kernel, out_shape=[slab] * 4 + [jax.ShapeDtypeStruct(...  43.1 us
    pallas_call x1, Pallas kernels, on_device(): pl.pallas_call(finish_kernel, out_shape=[slab] * 4 + [row] * 2, in_specs=...  2.21 us

profile of v3, /device:TPU:1, one launch (start us, length us, event | category | flops | bytes accessed | tf_op | source)
XLA Modules:
  0.0 46.7 jit_solution(11150481874026677425)
XLA Ops:
  0.6 0.0 copy-start.3
  0.6 0.0 copy-start
  0.7 0.0 copy-start.1
  0.7 0.0 copy-start.2
  0.7 0.6 %copy-done.3 = s32[1,64]{1,0:T(1,128)S(1)} copy-done((s32[1,64]{1,0:T(1,128)S(1)}, s32[1,64]{1,0:T(1,128)}, u32[]{:S(2)}) %copy-start.3) | copy-done | bytes 280
  1.3 0.0 copy-done
  1.3 0.0 copy-done.1
  1.3 0.0 copy-done.2
  1.3 43.1 %attend.1 = (bf16[1,256,1536]{2,1,0:T(8,128)(2,1)S(1)}, bf16[1,256,1536]{2,1,0:T(8,128)(2,1)S(1)}, bf16[1,256,1536]{2,1,0:T(8,128)(2,1)S(1)}, bf16[1,256,1536]{2,1,0:T(8,128)(2,1)S(1)}, f32[8,128]{1,0:T(8,128)S(1)}) custom-call(bf16[1,256,1536]{2,1,0:T(8,128)(2,1)} %q_hbm.1, bf16[1,256,1536]{2,1,0:T(8,128)(2,1)} %k_hbm.1, bf16[1,256,1536]{2,1,0:T(8,128)(2,1)} %v_hbm.1, ...), custom_call_target="tpu_custom_call" | custom-call | tf_op jit(solution)/shard_map/attend/pallas_call | solution.py:503
  44.5 2.2 %finish.1 = (bf16[1,256,1536]{2,1,0:T(8,128)(2,1)}, bf16[1,256,1536]{2,1,0:T(8,128)(2,1)}, bf16[1,256,1536]{2,1,0:T(8,128)(2,1)}, bf16[1,256,1536]{2,1,0:T(8,128...) custom-call(bf16[1,256,1536]{2,1,0:T(8,128)(2,1)S(1)} %get-tuple-element.17.refs_0_, ...), custom_call_target="tpu_custom_call" | custom-call | tf_op jit(solution)/shard_map/finish/pallas_call | solution.py:553
Async XLA Ops:
  0.6 0.7 %copy-start.3 = (s32[1,64]{1,0:T(1,128)S(1)}, s32[1,64]{1,0:T(1,128)}, u32[]{:S(2)}) copy-start(s32[1,64]{1,0:T(1,128)} %starts_any.1) | copy-start | bytes 772
  0.6 0.7 %copy-start = (f32[128]{0:T(128)S(1)}, f32[128]{0:T(128)}, u32[]{:S(2)}) copy-start(f32[128]{0:T(128)} %param.12) | copy-start | bytes 1540
  0.7 0.7 %copy-start.1 = (f32[128]{0:T(128)S(1)}, f32[128]{0:T(128)}, u32[]{:S(2)}) copy-start(f32[128]{0:T(128)} %param.13) | copy-start | bytes 1540
  0.7 0.7 %copy-start.2 = (s32[1,16]{1,0:T(1,128)S(1)}, s32[1,16]{1,0:T(1,128)}, u32[]{:S(2)}) copy-start(s32[1,16]{1,0:T(1,128)} %frames_any.1) | copy-start | bytes 196

commit v4 on v3

--- a/solution.py
+++ b/solution.py
@@ -67,7 +67,7 @@
     q_gain, k_gain, frames, starts, raw, halo, qn_own, kn_own, acc, stage, bias_f, bias_b,
     stat_cols, stat_mine, stat_halo, gain_acc, part, ring_in, clip_in, total,
     small_sem, load_sem, out_sem, send_sem, recv_sem, stat_send, stat_recv,
-    ready, ring_send, ring_recv, clip_send, clip_recv, total_send, total_recv,
+    ready, ring_send, ring_recv, clip_send, clip_recv, total_send, total_recv, own_sem,
 ):
     me = lax.axis_index("tm")
     clip = lax.axis_index("clip")
@@ -320,7 +320,7 @@
     send_far((3,), 1)
 
     for g in range(2, PACKETS):
-        send_far((2, 3), g)
+        send_far((3, 2), g)
 
     for n in range(FULL, PACKETS):
         out_copy(att_out, 0, n).start()
@@ -335,7 +335,7 @@
 
     def to_all(i):
         return pltpu.make_async_remote_copy(
-            src_ref=total, dst_ref=total, send_sem=total_send.at[i], recv_sem=total_recv,
+            src_ref=total, dst_ref=gains_out, send_sem=total_send.at[i], recv_sem=total_recv,
             device_id={"tm": i}, device_id_type=MESH,
         )
 
@@ -352,6 +352,9 @@
             def _():
                 to_clip(c, clip).start()
 
+    def own_total():
+        return pltpu.make_async_copy(total, gains_out, own_sem)
+
     def share_total():
         for c in range(N_CLIP):
 
@@ -365,14 +368,17 @@
         total[...] = everything
         for i in range(1, N_TM):
             to_all(i).start()
-
-    def backward_terms(side, local, g):
+        own_total().start()
+
+    def backward_terms(side, local, g, between=None):
         at = cols(g * PER + local)
         qn = halo[side, 3, :, at]
-        grads = halo[side, 2, :, at]
         logs = stat_halo[side, g, pl.ds(2 * local, 1), :]
         delta = stat_halo[side, g, pl.ds(2 * local + 1, 1), :]
         probs = jnp.exp2(dot(kn_own[:, at], qn, NT) * SCALE + bias_b[side] - logs)
+        if between is not None:
+            between()
+        grads = halo[side, 2, :, at]
         slopes = dot(raw[2, :, at], grads, NT)
         change = (probs * (slopes - delta)).astype(jnp.bfloat16)
         return (
@@ -387,9 +393,9 @@
         acc[1, :, at] = dv
         return g
 
-    def far_head(local, g):
+    def far_head(local, g, between=None):
         at = cols(g * PER + local)
-        dk, dv = backward_terms(1, local, g)
+        dk, dv = backward_terms(1, local, g, between)
         rough = raw[1, :, at].astype(jnp.float32)
         stage[2, :, at] = norm_back(rough, inv_rms(rough), gain_k, dk * ROOT).astype(jnp.bfloat16)
         stage[3, :, at] = dv.astype(jnp.bfloat16)
@@ -445,8 +451,8 @@
         out_copy(dv_out, 3, n).wait()
 
     for local in range(PER):
-        receive_far((2, 3), FULL + local)
-        far_head(local, FULL)
+        receive_far((3,), FULL + local)
+        far_head(local, FULL, lambda: receive_far((2,), FULL + local))
         out_copy(dk_out, 2, FULL + local).start()
         out_copy(dv_out, 3, FULL + local).start()
 
@@ -472,12 +478,11 @@
 
         for i in range(1, N_TM):
             to_all(i).wait_send()
+        own_total().wait()
 
     @pl.when(me > 0)
     def _():
         to_all(0).wait_recv()
-
-    gains_out[...] = total[...]
 
 
 def finish_kernel(*refs):
@@ -504,7 +509,7 @@
         main_kernel,
         out_shape=[slab] * 4 + [jax.ShapeDtypeStruct((8, HD), f32)],
         in_specs=[any_spec] * 8,
-        out_specs=[any_spec] * 4 + [vmem_spec],
+        out_specs=[any_spec] * 5,
         scratch_shapes=[
             pltpu.VMEM((1, HD), f32),
             pltpu.VMEM((1, HD), f32),
@@ -540,6 +545,7 @@
             dma((N_CLIP,)),
             dma((N_TM,)),
             dma,
+            dma,
         ],
         compiler_params=pltpu.CompilerParams(
             collective_id=0, has_side_effects=True, vmem_limit_bytes=203 * 2**18

time: 46.9 us -> 47 us (level)
  no operation moved by 1% of the time
where the time goes in v4:
time: 47 us; the launch traced here: 46.7 us
  Pallas kernels  45.4 us (97%)
  between operations  0.68 us (1%)
  local copies, waits for them, and re-layouts  0.67 us (1%)
    pallas_call x1, Pallas kernels, on_device(): pl.pallas_call(main_kernel, out_shape=[slab] * 4 + [jax.ShapeDtypeStruct(...  43.1 us
    pallas_call x1, Pallas kernels, on_device(): pl.pallas_call(finish_kernel, out_shape=[slab] * 4 + [row] * 2, in_specs=...  2.21 us

profile of v4, /device:TPU:1, one launch (start us, length us, event | category | flops | bytes accessed | tf_op | source)
XLA Modules:
  0.0 46.7 jit_solution(3600366852330092490)
XLA Ops:
  0.6 0.0 copy-start.3
  0.6 0.0 copy-start
  0.7 0.0 copy-start.1
  0.7 0.0 copy-start.2
  0.7 0.6 %copy-done.3 = s32[1,64]{1,0:T(1,128)S(1)} copy-done((s32[1,64]{1,0:T(1,128)S(1)}, s32[1,64]{1,0:T(1,128)}, u32[]{:S(2)}) %copy-start.3) | copy-done | bytes 280
  1.3 0.0 copy-done
  1.3 0.0 copy-done.1
  1.3 0.0 copy-done.2
  1.3 43.1 %attend.1 = (bf16[1,256,1536]{2,1,0:T(8,128)(2,1)S(1)}, bf16[1,256,1536]{2,1,0:T(8,128)(2,1)S(1)}, bf16[1,256,1536]{2,1,0:T(8,128)(2,1)S(1)}, bf16[1,256,1536]{2,1,0:T(8,128)(2,1)S(1)}, f32[8,128]{1,0:T(8,128)S(1)}) custom-call(bf16[1,256,1536]{2,1,0:T(8,128)(2,1)} %q_hbm.1, bf16[1,256,1536]{2,1,0:T(8,128)(2,1)} %k_hbm.1, bf16[1,256,1536]{2,1,0:T(8,128)(2,1)} %v_hbm.1, ...), custom_call_target="tpu_custom_call" | custom-call | tf_op jit(solution)/shard_map/attend/pallas_call | solution.py:508
  44.5 2.2 %finish.1 = (bf16[1,256,1536]{2,1,0:T(8,128)(2,1)}, bf16[1,256,1536]{2,1,0:T(8,128)(2,1)}, bf16[1,256,1536]{2,1,0:T(8,128)(2,1)}, bf16[1,256,1536]{2,1,0:T(8,128...) custom-call(bf16[1,256,1536]{2,1,0:T(8,128)(2,1)S(1)} %get-tuple-element.17.refs_0_, ...), custom_call_target="tpu_custom_call" | custom-call | tf_op jit(solution)/shard_map/finish/pallas_call | solution.py:559
Async XLA Ops:
  0.6 0.7 %copy-start.3 = (s32[1,64]{1,0:T(1,128)S(1)}, s32[1,64]{1,0:T(1,128)}, u32[]{:S(2)}) copy-start(s32[1,64]{1,0:T(1,128)} %starts_any.1) | copy-start | bytes 772
  0.6 0.7 %copy-start = (f32[128]{0:T(128)S(1)}, f32[128]{0:T(128)}, u32[]{:S(2)}) copy-start(f32[128]{0:T(128)} %param.12) | copy-start | bytes 1540
  0.7 0.7 %copy-start.1 = (f32[128]{0:T(128)S(1)}, f32[128]{0:T(128)}, u32[]{:S(2)}) copy-start(f32[128]{0:T(128)} %param.13) | copy-start | bytes 1540
  0.7 0.7 %copy-start.2 = (s32[1,16]{1,0:T(1,128)S(1)}, s32[1,16]{1,0:T(1,128)}, u32[]{:S(2)}) copy-start(s32[1,16]{1,0:T(1,128)} %frames_any.1) | copy-start | bytes 196
